TPU v7x, 32 devices: a whole 2x2x4 slice. The times are simulated.
32 devices in a mesh: blk: 4 (over y, x), clip: 8 (over z, core).
Axes of the slice: x: 2, y: 2, z: 4, core: 2. Of those that a mesh axis runs over, the one named last changes fastest.
Arguments:
- query_rows: bfloat16 [8, 768, 3072], P('clip', 'blk'), may hold values from -5.2 to 5.2
- key_rows: bfloat16 [8, 768, 3072], P('clip', 'blk'), may hold values from -5.2 to 5.2
- value_rows: bfloat16 [8, 768, 3072], P('clip', 'blk'), may hold values from -15 to 15
- residual: bfloat16 [8, 768, 3072], P('clip', 'blk'), may hold values from -12 to 12
- query_tangent: bfloat16 [8, 768, 3072], P(None, ('blk', 'clip')), may hold values from -6 to 6
- key_tangent: bfloat16 [8, 768, 3072], P(None, ('blk', 'clip')), may hold values from -6 to 6
- value_tangent: bfloat16 [8, 768, 3072], P(None, ('blk', 'clip')), may hold values from -15 to 15
- velocity: bfloat16 [8, 768, 3072], P(None, ('blk', 'clip')), may hold values from -12 to 12
- clip_slot: int32 [8], replicated, may hold values from 0 to 7, each once
- token_slot: int32 [32, 24], P(('blk', 'clip')), may hold values from 0 to 23, each once within a row
- clip_time: float32 [8], P('clip'), may hold values from 0.2 to 1.4
Outputs:
- attention_out: bfloat16 [8, 768, 3072], P('clip', 'blk')
- attention_tangent: bfloat16 [8, 768, 3072], P('clip', 'blk')
- target: bfloat16 [8, 768, 3072], P('clip', 'blk')
Inputs may be any that keep to these rules, and one draw needn't show every extreme that they name: `clip_slot`: a permutation: every clip has one teacher row. `token_slot`: every row is a permutation of the 24 positions of its run.
All inputs are finite; a program needn't handle non-finite values.
Results may differ from a plain program's by a relative error of at most 0.02.
Values may be sent and summed in bfloat16 or wider, within the bound.
A program may use at most 256 MiB of HBM per device.

v0:
```python
import jax
import jax.numpy as jnp
from jax import lax
from jax.sharding import PartitionSpec as P

HEAD_DIM = 128


sigma_data = 0.5
norm_offset = 0.1


def student_order(teacher, clip_slot, token_slot):
    by_clip = jnp.take(teacher, clip_slot, axis=0)
    return jnp.take(by_clip, token_slot[0], axis=1)


def teacher_streams(reordered):
    return (
        lax.all_to_all(reordered[0], "clip", split_axis=0, concat_axis=1, tiled=True),
        lax.all_to_all(reordered[1], "clip", split_axis=0, concat_axis=1, tiled=True),
        lax.all_to_all(reordered[2], "clip", split_axis=0, concat_axis=1, tiled=True),
        lax.all_to_all(reordered[3], "clip", split_axis=0, concat_axis=1, tiled=True),
    )


def local(
    query_rows,
    key_rows,
    value_rows,
    residual,
    query_tangent,
    key_tangent,
    value_tangent,
    velocity,
    clip_slot,
    token_slot,
    clip_time,
):
    reordered = tuple(
        (
            student_order(teacher, clip_slot, token_slot)
            for teacher in (query_tangent, key_tangent, value_tangent, velocity)
        )
    )
    tok_count = query_rows.shape[1]
    width_all = query_rows.shape[2]
    head_count = width_all // HEAD_DIM

    def split_heads(feature_rows):
        return feature_rows.reshape(tok_count, head_count, HEAD_DIM)

    query_dot, key_dot, value_dot, velocity_rows = teacher_streams(reordered)
    student = tuple(
        (
            split_heads(feature_rows)
            for feature_rows in (query_rows, key_rows, value_rows, query_dot, key_dot, value_dot)
        )
    )
    queries, keys_own, values_own, queries_dot, keys_dot_own, values_dot_own = student
    score_scale = HEAD_DIM ** (-0.5)
    running_max = jnp.full((tok_count, head_count), -1e30, jnp.float32)
    keys_piece = lax.all_gather(keys_own, "blk", axis=0, tiled=True)
    keys_dot_piece = lax.all_gather(keys_dot_own, "blk", axis=0, tiled=True)
    values_piece = lax.all_gather(values_own, "blk", axis=0, tiled=True)
    values_dot_piece = lax.all_gather(values_dot_own, "blk", axis=0, tiled=True)
    scores = (
        jnp.einsum("qhd,khd->qhk", queries, keys_piece, preferred_element_type=jnp.float32)
        * score_scale
    )
    score_dot = (
        jnp.einsum("qhd,khd->qhk", queries_dot, keys_piece, preferred_element_type=jnp.float32)
        + jnp.einsum("qhd,khd->qhk", queries, keys_dot_piece, preferred_element_type=jnp.float32)
    ) * score_scale
    new_max = jnp.maximum(running_max, jnp.max(scores, axis=2))
    weights = jnp.exp(scores - new_max[:, :, None])
    weighted = weights * score_dot
    both_values = jnp.concatenate((values_piece, values_dot_piece), axis=2)
    mixed = jnp.einsum(
        "qhk,khe->qhe",
        weights.astype(jnp.bfloat16),
        both_values,
        preferred_element_type=jnp.float32,
    )
    carried = jnp.einsum(
        "qhk,khd->qhd",
        weighted.astype(jnp.bfloat16),
        values_piece,
        preferred_element_type=jnp.float32,
    )
    final_state = (new_max, jnp.sum(weights, axis=2), jnp.sum(weighted, axis=2), mixed, carried)
    row_total = final_state[1][:, :, None]
    attention_full = final_state[3][:, :, :HEAD_DIM] / row_total
    tangent_full = (final_state[4] + final_state[3][:, :, HEAD_DIM:]) / row_total - final_state[2][
        :, :, None
    ] / row_total * attention_full
    attention = attention_full.astype(jnp.bfloat16)
    tangent = tangent_full.astype(jnp.bfloat16)
    attention_out = attention.reshape(1, tok_count, width_all)
    attention_tangent = tangent.reshape(1, tok_count, width_all)
    cosine = jnp.cos(clip_time[0])
    sine = jnp.sin(clip_time[0])
    mismatch = -cosine * cosine * (
        sigma_data * attention_out.astype(jnp.float32) - velocity_rows.astype(jnp.float32)
    ) - cosine * sine * (
        residual.astype(jnp.float32) + sigma_data * attention_tangent.astype(jnp.float32)
    )
    square_total = lax.psum(jnp.sum(mismatch * mismatch), "blk")
    mean_square = square_total / (lax.axis_size("blk") * tok_count * width_all)
    target = (mismatch / (jnp.sqrt(mean_square) + norm_offset)).astype(jnp.bfloat16)
    return (attention_out, attention_tangent, target)


def solution(mesh):
    in_specs = (
        P("clip", "blk", None),
        P("clip", "blk", None),
        P("clip", "blk", None),
        P("clip", "blk", None),
        P(None, ("blk", "clip"), None),
        P(None, ("blk", "clip"), None),
        P(None, ("blk", "clip"), None),
        P(None, ("blk", "clip"), None),
        P(),
        P(("blk", "clip"), None),
        P("clip"),
    )
    out_specs = (P("clip", "blk", None), P("clip", "blk", None), P("clip", "blk", None))
    return jax.shard_map(local, mesh=mesh, in_specs=in_specs, out_specs=out_specs, check_vma=False)
```

profile of v0, /device:TPU:0, one launch (start us, length us, event | category | flops | bytes accessed | tf_op | source)
XLA Modules:
  0.0 297.1 jit_solution(9990005621164618715)
XLA Ops:
  7.2 0.0 all-gather.9.cloned.1.call-start
  7.2 1.6 copy.62
  8.8 1.3 copy.49
  10.1 0.0 all-gather.9.cloned.1.call-update
  10.1 0.0 all-gather.11.cloned.1.call-start
  10.2 0.6 copy-done.18
  10.8 0.6 gather_fusion.2
  11.4 0.6 copy-done.11
  12.0 0.6 gather_fusion.4
  12.7 1.9 gather_fusion.6
  14.6 2.9 gather_fusion
  17.5 3.1 %broadcast_select_fusion = (bf16[8,24,3072]{2,1,0:T(8,128)(2,1)}, bf16[8,24,3072]{2,1,0:T(8,128)(2,1)S(1)}, bf16[8,24,3072]{2,1,0:T(8,128)(2,1)S(1)}, bf16[8,24,3072]{2,1,0:T(8,128)(2,1)}) fusion(bf16[8,24,3072]{2,1,0:T(8,128)(2,1)S(1)} %gather_fusion.6, pred[8]{0:T(512)(128)(4,1)S(1)} %compare_and_fusion.1, bf16[8,24,3072]{2,1,0:T(8,128)(2,1)S(1)} %gather_fusion.2, ...), kind=kLoop, calls=%fused_computation.41 | loop fusion | flops 2359296 | bytes 9437192 | tf_op jit(solution)/shard_map/jit(_take)/select_n | solution.py:14
  20.6 0.7 copy.52
  21.3 1.7 copy.55
  23.0 0.6 gather_fusion.3
  23.6 2.0 gather_fusion.5
  25.6 1.7 copy.60
  27.3 1.9 gather_fusion.7
  29.2 2.9 copy.46
  32.1 2.9 gather_fusion.1
  35.1 3.3 %select_bitcast_fusion = (bf16[8,24,3072]{2,0,1:T(8,128)(2,1)}, bf16[8,24,3072]{2,0,1:T(8,128)(2,1)}, bf16[8,24,3072]{2,0,1:T(8,128)(2,1)S(1)}, bf16[8,24,3072]{2,0,1:T(8,128)(2,1)}) fusion(bf16[24,8,3072]{2,1,0:T(8,128)(2,1)S(1)} %gather_fusion.7, pred[24]{0:T(512)(128)(4,1)S(1)} %compare_and_fusion, bf16[24,8,3072]{2,1,0:T(8,128)(2,1)S(1)} %gather_fusion.3, ...), kind=kLoop, calls=%fused_computation.37 | loop fusion | flops 2359296 | bytes 9437208 | tf_op jit(solution)/shard_map/jit(_take)/select_n | solution.py:15
  38.4 0.7 copy.56
  39.0 35.7 %all_to_all.16 = bf16[8,24,3072]{2,1,0:T(8,128)(2,1)S(1)} all-to-all(bf16[8,24,3072]{2,1,0:T(8,128)(2,1)S(1)} %copy.56), channel_id=1, replica_groups=mesh['blk'=4,'clip'=8] {'clip'}, dimensions={0} | all-to-all | bytes 2359296 | tf_op jit(solution)/shard_map/all_to_all | solution.py:21
  74.7 0.2 copy.67
  74.9 1.3 copy.57
  76.2 0.0 all-gather.11.cloned.1.call-update
  76.2 0.0 all-gather.5.cloned.1.call-start
  76.3 1.2 copy-done.13
  77.5 0.2 copy.64
  77.7 1.3 copy.45
  79.0 0.0 all-gather.7.cloned.1.call-start
  79.1 1.2 copy-done.8
  80.3 0.7 copy.47
  80.9 31.8 %all_to_all.17 = bf16[8,24,3072]{2,1,0:T(8,128)(2,1)S(1)} all-to-all(bf16[8,24,3072]{2,1,0:T(8,128)(2,1)S(1)} %copy.47), channel_id=1, replica_groups=mesh['blk'=4,'clip'=8] {'clip'}, dimensions={0} | all-to-all | bytes 2359296 | tf_op jit(solution)/shard_map/all_to_all | solution.py:22
  112.7 0.2 copy.65
  112.9 1.3 copy.48
  114.2 1.2 copy-done.7
  115.5 1.7 copy.53
  117.2 3.7 %all-to-all-start.1 = ((bf16[8,24,3072]{2,1,0:T(8,128)(2,1)}), bf16[8,24,3072]{2,1,0:T(8,128)(2,1)S(1)}, u32[]{:S(2)}, u32[]{:S(2)}) async-start(bf16[8,24,3072]{2,1,0:T(8,128)(2,1)} %copy.53), calls=%async_computation.1 | async-start | bytes 2359296 | tf_op jit(solution)/shard_map/all_to_all | solution.py:20
  121.7 0.2 copy.63
  121.9 1.1 copy-done.6
  122.9 1.7 copy.61
  124.6 25.6 %all-to-all-done.1 = bf16[8,24,3072]{2,1,0:T(8,128)(2,1)S(1)} async-done(((bf16[8,24,3072]{2,1,0:T(8,128)(2,1)}), bf16[8,24,3072]{2,1,0:T(8,128)(2,1)S(1)}, u32[]{:S(2)}, u32[]{:S(2)}) %all-to-all-start.1) | async-done | bytes 1179680 | tf_op jit(solution)/shard_map/all_to_all | solution.py:20
  150.2 1.0 copy-done.10
  151.2 3.7 %all-to-all-start.3 = ((bf16[8,24,3072]{2,1,0:T(8,128)(2,1)}), bf16[8,24,3072]{2,1,0:T(8,128)(2,1)S(1)}, u32[]{:S(2)}, u32[]{:S(2)}) async-start(bf16[8,24,3072]{2,1,0:T(8,128)(2,1)} %copy.61), calls=%async_computation.3 | async-start | bytes 2359296 | tf_op jit(solution)/shard_map/all_to_all | solution.py:23
  154.9 1.5 copy.66
  156.4 0.0 all-gather.9.cloned.1.call-done
  156.5 4.4 %bitcast_reduce_fusion = (f32[192,24]{0,1:T(8,128)S(1)}, f32[24,768,192]{1,2,0:T(8,128)S(1)}) fusion(bf16[768,24,128]{2,0,1:T(8,128)(2,1)} %all-gather.9.cloned.1.call-done, bf16[192,24,128]{2,1,0:T(8,128)(2,1)S(1)} %bitcast.76), kind=kOutput, calls=%fused_computation.12 | convolution fusion | flops 913042944 | bytes 20072448 | tf_op jit(solution)/shard_map/qhd,khd->qhk/dot_general | solution.py:68
  160.9 13.1 %fusion.26 = f32[24,192,768]{2,1,0:T(8,128)} fusion(bf16[768,24,128]{2,0,1:T(8,128)(2,1)} %all-gather.9.cloned.1.call-done, bf16[192,24,128]{2,1,0:T(8,128)(2,1)S(1)} %bitcast.78), kind=kOutput, calls=%fused_computation.35 | convolution fusion | flops 905969664 | bytes 20054016 | tf_op jit(solution)/shard_map/qhd,khd->qhk/dot_general | solution.py:72
  174.0 3.2 %fusion.7 = f32[192,24]{0,1:T(8,128)S(1)} fusion(f32[24,768,192]{1,2,0:T(8,128)S(1)} %get-tuple-element.14, f32[192,24]{0,1:T(8,128)S(1)} %broadcast_maximum_fusion), kind=kLoop, calls=%fused_computation.18 | loop fusion | flops 10612224 | bytes 14192640 | tf_op jit(solution)/shard_map/reduce_sum | solution.py:91
  177.3 0.0 all-gather.11.cloned.1.call-done
  177.3 16.1 %fusion.34 = (f32[192,24]{0,1:T(8,128)S(1)}, bf16[192,24,768]{2,0,1:T(8,128)(2,1)}) fusion(bf16[768,24,128]{2,0,1:T(8,128)(2,1)} %all-gather.11.cloned.1.call-done, bf16[192,24,128]{2,1,0:T(8,128)(2,1)S(1)} %bitcast.77, f32[24,192,768]{2,1,0:T(8,128)} %fusion.26, f32[192,24]{0,1:T(8,128)} %copy-done.15, f32[24,768,192]{1,2,0:T(8,128)} %copy-done.2), kind=kOutput, calls=%fused_computation.58 | convolution fusion | flops 930737664 | bytes 41324544 | tf_op jit(solution)/shard_map/qhd,khd->qhk/dot_general | solution.py:73
  193.4 56.8 %all-gather.7.cloned.1.call-done = bf16[768,24,128]{2,0,1:T(8,128)(2,1)} async-done(((bf16[192,24,128]{2,0,1:T(8,128)(2,1)}), bf16[768,24,128]{2,0,1:T(8,128)(2,1)}) %all-gather.7.cloned.1.call-update) | async-done | bytes 4718608 | tf_op jit(solution)/shard_map/all_gather | solution.py:66
  250.1 9.5 %fusion.19 = f32[192,24,256]{2,0,1:T(8,128)S(1)} fusion(bf16[768,24,128]{2,0,1:T(8,128)(2,1)} %all-gather.7.cloned.1.call-done, bf16[768,24,128]{2,0,1:T(8,128)(2,1)} %all-gather.5.cloned.1.call-done, f32[24,768,192]{1,2,0:T(8,128)} %copy-done.2, f32[192,24]{0,1:T(8,128)S(1)} %copy-done.16), kind=kOutput, calls=%fused_computation.34 | convolution fusion | flops 1841430528 | bytes 28329984 | tf_op jit(solution)/shard_map/qhk,khe->qhe/dot_general | solution.py:79
  259.7 0.2 copy-done.5
  259.9 5.5 %fusion.18 = bf16[192,24,128]{2,0,1:T(8,128)(2,1)S(1)} fusion(f32[192,24,256]{2,0,1:T(8,128)S(1)} %fusion.19, bf16[768,24,128]{2,0,1:T(8,128)(2,1)} %all-gather.5.cloned.1.call-done, bf16[192,24,768]{2,0,1:T(8,128)(2,1)S(1)} %copy-done.5, f32[192,24]{0,1:T(8,128)S(1)} %div.34, f32[192,24]{0,1:T(8,128)S(1)} %fusion.7), kind=kOutput, calls=%fused_computation.33 | convolution fusion | flops 909508608 | bytes 17731584 | tf_op jit(solution)/shard_map/qhk,khd->qhd/dot_general | solution.py:85
  265.4 0.8 copy.59
  266.2 0.5 reshape.128
  266.7 2.5 fusion.31
  269.3 1.8 copy.51
  271.1 2.2 reshape.125
  273.3 3.3 %multiply_reduce_fusion = f32[]{:T(128)} fusion(bf16[1,192,3072]{2,1,0:T(8,128)(2,1)S(1)} %reshape.128, bf16[1,192,3072]{2,1,0:T(8,128)(2,1)} %param.18, f32[]{:T(128)S(6)} %mul.81, bf16[1,192,3072]{2,1,0:T(8,128)(2,1)S(1)} %reshape.125, f32[]{:T(128)S(6)} %mul.77, bf16[1,192,3072]{2,1,0:T(8,128)(2,1)S(1)} %bitcast.74), kind=kLoop, calls=%fused_computation.32 | loop fusion | flops 7667711 | bytes 4718604 | tf_op jit(solution)/shard_map/reduce_sum | solution.py:108
  276.6 9.5 %psum.7 = f32[]{:T(128)} all-reduce(f32[]{:T(128)} %multiply_reduce_fusion), channel_id=1, replica_groups=mesh['blk'=4,'clip'=8] {'blk'}, use_global_device_ids=true, to_apply=%region_4.7 | all-reduce | flops 1 | bytes 8 | tf_op jit(solution)/shard_map/psum | solution.py:108
  286.9 3.7 %divide_convert_fusion = bf16[1,192,3072]{2,1,0:T(8,128)(2,1)} fusion(f32[]{:T(128)S(6)} %add.23, bf16[1,192,3072]{2,1,0:T(8,128)(2,1)S(1)} %reshape.128, bf16[1,192,3072]{2,1,0:T(8,128)(2,1)} %param.18, f32[]{:T(128)S(6)} %mul.81, bf16[1,192,3072]{2,1,0:T(8,128)(2,1)} %copy-done.4, f32[]{:T(128)S(6)} %mul.77, bf16[1,192,3072]{2,1,0:T(8,128)(2,1)S(1)} %bitcast.75), kind=kLoop, calls=%fused_computation.31 | loop fusion | flops 7667712 | bytes 5898252 | tf_op jit(solution)/shard_map/convert_element_type | solution.py:110
  (44 shorter events, 0.2 us)
Async XLA Ops:
  7.2 3.6 %copy-start = (bf16[8,24,3072]{2,1,0:T(8,128)(2,1)S(1)}, bf16[8,24,3072]{2,1,0:T(8,128)(2,1)}, u32[]{:S(2)}) copy-start(bf16[8,24,3072]{2,1,0:T(8,128)(2,1)} %param.19) | copy-start | bytes 3538948
  7.2 149.3 %all-gather.9.cloned.1.call-start = ((), (), s32[]{:S(2)}) async-start(), calls=%async_computation.6 | async-start | bytes 5898240 | tf_op jit(solution)/shard_map/all_gather | solution.py:63
  10.1 0.7 copy-start.18
  10.1 167.2 %all-gather.11.cloned.1.call-start = ((), (), s32[]{:S(2)}) async-start(), calls=%async_computation.7 | async-start | bytes 5898240 | tf_op jit(solution)/shard_map/all_gather | solution.py:64
  10.8 1.3 copy-start.11
  21.3 1.7 copy-start.19
  23.6 2.0 copy-start.9
  76.2 1.3 copy-start.13
  76.2 117.1 %all-gather.5.cloned.1.call-start = ((), (), s32[]{:S(2)}) async-start(), calls=%async_computation.4 | async-start | bytes 5898240 | tf_op jit(solution)/shard_map/all_gather | solution.py:65
  79.0 1.3 copy-start.8
  79.0 171.1 %all-gather.7.cloned.1.call-start = ((), (), s32[]{:S(2)}) async-start(), calls=%async_computation.5 | async-start | bytes 5898240 | tf_op jit(solution)/shard_map/all_gather | solution.py:66
  114.2 1.3 copy-start.7
  117.2 4.5 %copy-start.14 = (bf16[1,192,3072]{2,1,0:T(8,128)(2,1)S(1)}, bf16[1,192,3072]{2,1,0:T(8,128)(2,1)}, u32[]{:S(2)}) copy-start(bf16[1,192,3072]{2,1,0:T(8,128)(2,1)} %param.15) | copy-start | bytes 3538948
  117.2 33.0 %all-to-all-start.1 = ((bf16[8,24,3072]{2,1,0:T(8,128)(2,1)}), bf16[8,24,3072]{2,1,0:T(8,128)(2,1)S(1)}, u32[]{:S(2)}, u32[]{:S(2)}) async-start(bf16[8,24,3072]{2,1,0:T(8,128)(2,1)} %copy.53), calls=%async_computation.1 | async-start | bytes 2359296 | tf_op jit(solution)/shard_map/all_to_all | solution.py:20
  121.7 1.3 copy-start.6
  150.2 1.0 copy-start.10
  151.2 122.1 %all-to-all-start.3 = ((bf16[8,24,3072]{2,1,0:T(8,128)(2,1)}), bf16[8,24,3072]{2,1,0:T(8,128)(2,1)S(1)}, u32[]{:S(2)}, u32[]{:S(2)}) async-start(bf16[8,24,3072]{2,1,0:T(8,128)(2,1)} %copy.61), calls=%async_computation.3 | async-start | bytes 2359296 | tf_op jit(solution)/shard_map/all_to_all | solution.py:23
  160.9 13.1 %copy-start.2 = (f32[24,768,192]{1,2,0:T(8,128)}, f32[24,768,192]{1,2,0:T(8,128)S(1)}, u32[]{:S(2)}) copy-start(f32[24,768,192]{1,2,0:T(8,128)S(1)} %get-tuple-element.14) | copy-start | bytes 42467332
  160.9 13.1 %copy-start.15 = (f32[192,24]{0,1:T(8,128)}, f32[192,24]{0,1:T(8,128)S(1)}, u32[]{:S(2)}) copy-start(f32[192,24]{0,1:T(8,128)S(1)} %broadcast_maximum_fusion) | copy-start | bytes 55300
  177.3 82.4 %copy-start.17 = (f32[192,24]{0,1:T(8,128)}, f32[192,24]{0,1:T(8,128)S(1)}, u32[]{:S(2)}) copy-start(f32[192,24]{0,1:T(8,128)S(1)} %fusion.7) | copy-start | bytes 55300
  177.3 72.9 %copy-start.16 = (f32[192,24]{0,1:T(8,128)S(1)}, f32[192,24]{0,1:T(8,128)}, u32[]{:S(2)}) copy-start(f32[192,24]{0,1:T(8,128)} %copy-done.15) | copy-start | bytes 55300
  250.1 9.8 %copy-start.5 = (bf16[192,24,768]{2,0,1:T(8,128)(2,1)S(1)}, bf16[192,24,768]{2,0,1:T(8,128)(2,1)}, u32[]{:S(2)}) copy-start(bf16[192,24,768]{2,0,1:T(8,128)(2,1)} %get-tuple-element.16) | copy-start | bytes 21233668
  259.6 5.8 %copy-start.12 = (f32[192,24,256]{2,0,1:T(8,128)}, f32[192,24,256]{2,0,1:T(8,128)S(1)}, u32[]{:S(2)}) copy-start(f32[192,24,256]{2,0,1:T(8,128)S(1)} %fusion.19) | copy-start | bytes 14155780
  266.7 20.1 %copy-start.3 = (bf16[1,192,3072]{2,1,0:T(8,128)(2,1)}, bf16[1,192,3072]{2,1,0:T(8,128)(2,1)S(1)}, u32[]{:S(2)}) copy-start(bf16[1,192,3072]{2,1,0:T(8,128)(2,1)S(1)} %reshape.128) | copy-start | bytes 3538948
  273.3 3.3 %copy-start.4 = (bf16[1,192,3072]{2,1,0:T(8,128)(2,1)}, bf16[1,192,3072]{2,1,0:T(8,128)(2,1)S(1)}, u32[]{:S(2)}) copy-start(bf16[1,192,3072]{2,1,0:T(8,128)(2,1)S(1)} %reshape.125) | copy-start | bytes 3538948
  286.9 3.7 %copy-start.1 = (bf16[8,24,3072]{2,1,0:T(8,128)(2,1)S(1)}, bf16[8,24,3072]{2,1,0:T(8,128)(2,1)}, u32[]{:S(2)}) copy-start(bf16[8,24,3072]{2,1,0:T(8,128)(2,1)} %param.19) | copy-start | bytes 3538948
Sparse Core Ops, SparseCore 0:
  10.4 59.7 all-gather.8
  76.4 55.9 all-gather.10
  134.2 57.0 all-gather.4
  193.0 57.0 all-gather.6
where the time goes:
time: 298 us; the launch traced here: 297 us
  waiting for transfers between devices  82.4 us (28%)
  blocking collectives  77 us (26%)
  matrix products  48.6 us (16%)
  local copies, waits for them, and re-layouts  46.6 us (16%)
  other arithmetic  19.2 us (6%)
  between operations  15.6 us (5%)
  starting transfers between devices  7.6 us (3%)
    all_gather x1, waiting for transfers between devices, local(): values_dot_piece = lax.all_gather(values_dot_own, 'blk', axis=0, tiled=True)  56.8 us
    all_to_all x1, blocking collectives, teacher_streams(): lax.all_to_all(reordered[1], 'clip', split_axis=0, concat_axis=1, tiled=T...  35.7 us
    all_to_all x1, blocking collectives, teacher_streams(): lax.all_to_all(reordered[2], 'clip', split_axis=0, concat_axis=1, tiled=T...  31.8 us
    all_to_all x1, waiting for transfers between devices, teacher_streams(): lax.all_to_all(reordered[0], 'clip', split_axis=0, concat_axis=1, tiled=T...  25.6 us
    dot_general x1, matrix products, local(): jnp.einsum('qhd,khd->qhk', queries, keys_dot_piece, preferred_element_typ...  16.1 us
    dot_general x1, matrix products, local(): jnp.einsum('qhd,khd->qhk', queries_dot, keys_piece, preferred_element_typ...  13.1 us
    unnamed x46, local copies, waits for them, and re-layouts  11 us
    psum x1, blocking collectives, local(): square_total = lax.psum(jnp.sum(mismatch * mismatch), 'blk')  9.54 us
  transfers between devices with their start and end apart: 6, of which 2 were waited for; matrix products, arithmetic and copies ran while one was open for 33% of the time, Pallas kernels for 0%

commit v1 on v0

v1 whole, which is shorter than its diff:
```python
import functools
import math

import jax
import jax.numpy as jnp
from jax import lax
from jax.experimental import pallas as pl
from jax.experimental.pallas import tpu as pltpu
from jax.sharding import PartitionSpec as P

HEAD_DIM = 128
SIGMA = 0.5
OFFSET = 0.1
MESH = pl.DeviceIdType.MESH
F32 = jnp.float32
BF16 = jnp.bfloat16


def kernel(
    nb, nc, hc, chunks,
    slot_ref, coef_ref, pick_ref,
    q_ref, k_ref, v_ref, res_ref,
    qt_ref, kt_ref, vt_ref, vel_ref,
    out_ref, tan_ref, target_ref,
    teach, teach_vel, send, recv, stud, dots, own_out, got_out, vel_send, vel_recv, resid, mism, goal,
    part, parts,
    load_sem, send_sem, recv_sem, stud_send, stud_recv, out_send, out_recv,
    vel_ssem, vel_rsem, part_send, part_recv, write_sem,
):
    n = nb * nc
    run = teach.shape[2]
    tok = q_ref.shape[1]
    width = q_ref.shape[2]
    seq = stud.shape[1]
    group_width = width // nb
    cw = hc * HEAD_DIM
    join = 16 // math.gcd(run, 16)
    my_b = lax.axis_index("blk")
    my_c = lax.axis_index("clip")
    me = my_b * nc + my_c

    loads = []
    for t, ref in enumerate((qt_ref, kt_ref, vt_ref)):
        loads.append(pltpu.make_async_copy(ref, teach.at[t], load_sem.at[t]))
    loads.append(pltpu.make_async_copy(vel_ref, teach_vel, load_sem.at[3]))
    loads.append(pltpu.make_async_copy(res_ref.at[0], resid, load_sem.at[4]))
    for load in loads:
        load.start()

    barrier = pltpu.get_barrier_semaphore()

    @pl.loop(1, n)
    def _(m):
        d = lax.rem(me + m, n)
        pl.semaphore_signal(barrier, inc=1, device_id=(d // nc, lax.rem(d, nc)), device_id_type=MESH)

    pick = pick_ref[...]

    def build(c, d):
        g, i = d // nc, lax.rem(d, nc)
        slot = slot_ref[i]
        col = pl.multiple_of(g * group_width + c * cw, 128)
        pieces = []
        for t in range(3):
            rows = jnp.dot(pick, teach[t, slot, :, pl.ds(col, cw)], preferred_element_type=F32)
            for hh in range(hc):
                pieces.append(rows[:, hh * HEAD_DIM:(hh + 1) * HEAD_DIM])
        spare = send.shape[2] - 3 * hc * run
        if spare:
            pieces.append(jnp.zeros((spare, HEAD_DIM), F32))
        send[c, d] = jnp.concatenate(pieces, axis=0).astype(BF16)

    def students(c):
        for s, ref in enumerate((q_ref, k_ref, v_ref)):
            for off in range(nb):
                g = lax.rem(my_b + off, nb)
                src = ref.at[0, :, pl.ds(pl.multiple_of(g * group_width + c * cw, 128), cw)]
                dst = stud.at[s, pl.ds(pl.multiple_of(my_b * tok, 16), tok), pl.ds(c * cw, cw)]
                if off == 0:
                    pltpu.make_async_copy(src, dst, stud_recv.at[c]).start()
                else:
                    pltpu.make_async_remote_copy(
                        src_ref=src, dst_ref=dst, send_sem=stud_send, recv_sem=stud_recv.at[c],
                        device_id=(g, my_c), device_id_type=MESH,
                    ).start()

    for load in loads[:3]:
        load.wait()
    pl.semaphore_wait(barrier, n - 1)

    for c in range(chunks):
        @pl.loop(1, n)
        def _(m):
            d = lax.rem(me + m, n)
            build(c, d)
            pltpu.make_async_remote_copy(
                src_ref=send.at[c, d], dst_ref=recv.at[c, me],
                send_sem=send_sem, recv_sem=recv_sem.at[c],
                device_id=(d // nc, lax.rem(d, nc)), device_id_type=MESH,
            ).start()

        build(c, me)
        pltpu.make_async_copy(send.at[c, me], recv.at[c, me], recv_sem.at[c]).start()
        students(c)

    loads[3].wait()

    def build_velocity(i):
        slot = slot_ref[i]
        rows = jnp.dot(pick, teach_vel[slot], preferred_element_type=F32)
        heads = [rows[:, h * HEAD_DIM:(h + 1) * HEAD_DIM] for h in range(width // HEAD_DIM)]
        vel_send[i] = jnp.concatenate(heads, axis=0).astype(BF16)

    @pl.loop(1, nc)
    def _(m):
        i = lax.rem(my_c + m, nc)
        build_velocity(i)
        pltpu.make_async_remote_copy(
            src_ref=vel_send.at[i], dst_ref=vel_recv.at[my_c],
            send_sem=vel_ssem, recv_sem=vel_rsem,
            device_id=(my_b, i), device_id_type=MESH,
        ).start()

    build_velocity(my_c)
    pltpu.make_async_copy(vel_send.at[my_c], vel_recv.at[my_c], vel_rsem).start()

    scale = HEAD_DIM ** (-0.5)
    tile = 256
    for c in range(chunks):
        pltpu.make_async_copy(recv.at[c], recv.at[c], recv_sem.at[c]).wait()
        waited = stud.at[:, :, pl.ds(c * cw, cw)]
        pltpu.make_async_copy(waited, waited, stud_recv.at[c]).wait()

        @pl.loop(0, n // join)
        def _(j):
            slabs = [recv[c, j * join + u].astype(F32) for u in range(join)]
            for t in range(3):
                for hh in range(hc):
                    at = (t * hc + hh) * run
                    rows = jnp.concatenate([slab[at:at + run] for slab in slabs], axis=0)
                    dots[t, hh, pl.ds(pl.multiple_of(j * (join * run), 16), join * run), :] = rows.astype(BF16)

        for hh in range(hc):
            lane = c * cw + hh * HEAD_DIM

            @pl.loop(0, seq // tile)
            def _(r):
                at = pl.ds(pl.multiple_of(r * tile, tile), tile)
                keys = stud[1, :, lane:lane + HEAD_DIM]
                both_keys = jnp.concatenate([keys, dots[1, hh]], axis=1)
                both_values = jnp.concatenate([stud[2, :, lane:lane + HEAD_DIM], dots[2, hh]], axis=1)
                query = stud[0, at, lane:lane + HEAD_DIM]
                both_queries = jnp.concatenate([dots[0, hh, at, :], query], axis=1)
                over = (((1,), (1,)), ((), ()))
                scores = lax.dot_general(query, keys, over, preferred_element_type=F32)
                score_dot = lax.dot_general(both_queries, both_keys, over, preferred_element_type=F32)
                top = jnp.max(scores, axis=1, keepdims=True)
                weights = jnp.exp2((scores - top) * (scale * math.log2(math.e)))
                weighted = weights * score_dot
                total = jnp.sum(weights, axis=1, keepdims=True)
                dot_total = jnp.sum(weighted, axis=1, keepdims=True) * scale
                mixed = jnp.dot(weights.astype(BF16), both_values, preferred_element_type=F32)
                carried = jnp.dot(
                    weighted.astype(BF16), both_values[:, :HEAD_DIM], preferred_element_type=F32
                )
                inverse = 1.0 / total
                attention = mixed[:, :HEAD_DIM] * inverse
                tangent = (carried * scale + mixed[:, HEAD_DIM:]) * inverse - (dot_total * inverse) * attention
                own_out[0, at, lane:lane + HEAD_DIM] = attention.astype(BF16)
                own_out[1, at, lane:lane + HEAD_DIM] = tangent.astype(BF16)

        for off in [*range(1, nb), 0]:
            b = lax.rem(my_b + off, nb)
            src = own_out.at[:, pl.ds(pl.multiple_of(b * tok, 16), tok), pl.ds(c * cw, cw)]
            dst = got_out.at[:, :, pl.ds(pl.multiple_of(my_b * group_width + c * cw, 128), cw)]
            if off == 0:
                pltpu.make_async_copy(src, dst, out_recv.at[c]).start()
            else:
                pltpu.make_async_remote_copy(
                    src_ref=src, dst_ref=dst, send_sem=out_send, recv_sem=out_recv.at[c],
                    device_id=(b, my_c), device_id_type=MESH,
                ).start()

    pltpu.make_async_copy(vel_recv, vel_recv, vel_rsem).wait()
    loads[4].wait()
    for c in range(chunks):
        waited = got_out.at[:, :, pl.ds(0, nb * cw)]
        pltpu.make_async_copy(waited, waited, out_recv.at[c]).wait()
    writes = [
        pltpu.make_async_copy(got_out.at[0], out_ref.at[0], write_sem.at[0]),
        pltpu.make_async_copy(got_out.at[1], tan_ref.at[0], write_sem.at[1]),
    ]
    for write in writes:
        write.start()

    square_cos, cos_sin = coef_ref[0], coef_ref[1]
    part[...] = jnp.zeros_like(part)

    @pl.loop(0, width // HEAD_DIM // join)
    def _(j):
        blocks = [
            vel_recv[p, pl.ds(pl.multiple_of(j * (join * run), 16), join * run), :].astype(F32)
            for p in range(nc)
        ]
        added = part[...]
        for u in range(join):
            at = pl.ds(pl.multiple_of((j * join + u) * HEAD_DIM, 128), HEAD_DIM)
            velocity = jnp.concatenate([block[u * run:(u + 1) * run] for block in blocks], axis=0)
            off = -square_cos * (SIGMA * got_out[0, :, at].astype(F32) - velocity) - cos_sin * (
                resid[:, at].astype(F32) + SIGMA * got_out[1, :, at].astype(F32)
            )
            mism[:, at] = off
            added = added + jnp.sum((off * off).reshape(tok // 8, 8, HEAD_DIM), axis=0)
        part[...] = added

    for off in range(1, nb):
        pltpu.make_async_remote_copy(
            src_ref=part, dst_ref=parts.at[off - 1], send_sem=part_send, recv_sem=part_recv,
            device_id=(lax.rem(my_b + off, nb), my_c), device_id_type=MESH,
        ).start()
    pltpu.make_async_copy(parts, parts, part_recv).wait()
    whole = part[...] + jnp.sum(parts[...], axis=0)
    mean_square = jnp.sum(whole, keepdims=True) / (nb * tok * width)
    factor = 1.0 / (jnp.sqrt(mean_square) + OFFSET)

    @pl.loop(0, width // HEAD_DIM)
    def _(h):
        at = pl.ds(pl.multiple_of(h * HEAD_DIM, 128), HEAD_DIM)
        goal[:, at] = (mism[:, at] * factor).astype(BF16)

    last = pltpu.make_async_copy(goal, target_ref.at[0], write_sem.at[2])
    last.start()

    pltpu.make_async_copy(parts, parts, part_send).wait()
    sent = recv.at[:, pl.ds(0, n - 1)]
    pltpu.make_async_copy(sent, sent, send_sem).wait()
    sent = stud.at[:, pl.ds(0, (nb - 1) * tok), :]
    pltpu.make_async_copy(sent, sent, stud_send).wait()
    sent = got_out.at[:, :, pl.ds(0, (nb - 1) * group_width)]
    pltpu.make_async_copy(sent, sent, out_send).wait()
    sent = vel_recv.at[pl.ds(0, nc - 1)]
    pltpu.make_async_copy(sent, sent, vel_ssem).wait()
    for write in writes:
        write.wait()
    last.wait()


def local(
    nb, nc,
    query_rows, key_rows, value_rows, residual,
    query_tangent, key_tangent, value_tangent, velocity,
    clip_slot, token_slot, clip_time,
):
    _, tok, width = query_rows.shape
    clips, run, _ = query_tangent.shape
    n = nb * nc
    seq = nb * tok
    own_heads = width // HEAD_DIM // nb
    hc = 2 if own_heads % 2 == 0 else 1
    chunks = own_heads // hc
    slab = -(-3 * hc * run // 16) * 16
    group_width = width // nb
    heads = width // HEAD_DIM
    cosine, sine = jnp.cos(clip_time[0]), jnp.sin(clip_time[0])
    coef = jnp.stack([cosine * cosine, cosine * sine])
    pick = (token_slot[0][:, None] == jnp.arange(run, dtype=jnp.int32)[None, :]).astype(BF16)
    out = jax.ShapeDtypeStruct((1, tok, width), BF16)
    anywhere = pl.BlockSpec(memory_space=pl.ANY)
    small = pl.BlockSpec(memory_space=pltpu.SMEM)
    dma = pltpu.SemaphoreType.DMA
    return pl.pallas_call(
        functools.partial(kernel, nb, nc, hc, chunks),
        out_shape=(out, out, out),
        in_specs=[small, small, pl.BlockSpec(memory_space=pltpu.VMEM)] + [anywhere] * 8,
        out_specs=(anywhere,) * 3,
        scratch_shapes=[
            pltpu.VMEM((3, clips, run, width), BF16),
            pltpu.VMEM((clips, run, width), BF16),
            pltpu.VMEM((chunks, n, slab, HEAD_DIM), BF16),
            pltpu.VMEM((chunks, n, slab, HEAD_DIM), BF16),
            pltpu.VMEM((3, seq, group_width), BF16),
            pltpu.VMEM((3, hc, seq, HEAD_DIM), BF16),
            pltpu.VMEM((2, seq, group_width), BF16),
            pltpu.VMEM((2, tok, width), BF16),
            pltpu.VMEM((nc, heads * run, HEAD_DIM), BF16),
            pltpu.VMEM((nc, heads * run, HEAD_DIM), BF16),
            pltpu.VMEM((tok, width), BF16),
            pltpu.VMEM((tok, width), F32),
            pltpu.VMEM((tok, width), BF16),
            pltpu.VMEM((8, HEAD_DIM), F32),
            pltpu.VMEM((nb - 1, 8, HEAD_DIM), F32),
            dma((5,)), dma, dma((chunks,)), dma, dma((chunks,)), dma, dma((chunks,)),
            dma, dma, dma, dma, dma((3,)),
        ],
        compiler_params=pltpu.CompilerParams(
            collective_id=0, has_side_effects=True, vmem_limit_bytes=56 * 1024 * 1024
        ),
        name="clip_attention",
    )(
        clip_slot, coef, pick,
        query_rows, key_rows, value_rows, residual,
        query_tangent, key_tangent, value_tangent, velocity,
    )


def solution(mesh):
    rows = P("clip", "blk", None)
    teacher = P(None, ("blk", "clip"), None)
    in_specs = (rows,) * 4 + (teacher,) * 4 + (P(), P(("blk", "clip"), None), P("clip"))
    return jax.shard_map(
        functools.partial(local, mesh.shape["blk"], mesh.shape["clip"]),
        mesh=mesh, in_specs=in_specs, out_specs=(rows,) * 3, check_vma=False,
    )
```

time: 298 us -> 130 us (0.44)
  Pallas kernels: 0 us -> 122 us
  waiting for transfers between devices: 82.4 us -> 0 us
  blocking collectives: 77 us -> 0 us
  matrix products: 48.6 us -> 0 us
  local copies, waits for them, and re-layouts: 46.6 us -> 5.17 us
  other arithmetic: 19.2 us -> 1.91 us
  between operations: 15.6 us -> 1.45 us
  starting transfers between devices: 7.6 us -> 0 us
    pallas_call x0 -> x1, Pallas kernels: none -> 122 us  [local(): pl.pallas_call(functools.partial(kernel, nb, nc, hc, chunks), out_shape=(...]
    all_to_all x2 -> x0, blocking collectives: 67.5 us -> none  [the longest x1 35.7 us: teacher_streams(): lax.all_to_all(reordered[1], 'clip', split_axis=0, concat_axis=1, tiled=T...]
    all_gather x4 -> x0, waiting for transfers between devices: 56.8 us -> none  [the longest x1 56.8 us: local(): values_dot_piece = lax.all_gather(values_dot_own, 'blk', axis=0, tiled=True)]
    dot_general x5 -> x0, matrix products: 48.6 us -> none  [the longest x1 16.1 us: local(): jnp.einsum('qhd,khd->qhk', queries, keys_dot_piece, preferred_element_typ...]
    all_to_all x2 -> x0, waiting for transfers between devices: 25.6 us -> none  [the longest x1 25.6 us: teacher_streams(): lax.all_to_all(reordered[0], 'clip', split_axis=0, concat_axis=1, tiled=T...]
    gather x8 -> x0, local copies, waits for them, and re-layouts: 13.5 us -> none  [the longest x4 7.44 us: student_order(): return jnp.take(by_clip, token_slot[0], axis=1)]
    select_n x8 -> x0, local copies, waits for them, and re-layouts: 11.6 us -> none  [the longest x4 6.95 us: student_order(): by_clip = jnp.take(teacher, clip_slot, axis=0)]
    psum x1 -> x0, blocking collectives: 9.54 us -> none  [local(): square_total = lax.psum(jnp.sum(mismatch * mismatch), 'blk')]
  transfers between devices with their start and end apart: 6 -> 0, of which waited for: 2 -> 0; matrix products, arithmetic and copies ran while one was open for 33% -> 0% of each run, Pallas kernels for 0% -> 0%
where the time goes in v1:
time: 130 us
  Pallas kernels  122 us (94%)
  local copies, waits for them, and re-layouts  5.17 us (4%)
  other arithmetic  1.91 us (1%)
  between operations  1.45 us (1%)
    pallas_call x1, Pallas kernels, local(): pl.pallas_call(functools.partial(kernel, nb, nc, hc, chunks), out_shape=(...  122 us
    unnamed x7, local copies, waits for them, and re-layouts  5.17 us

profile of v1, /device:TPU:0, one launch (start us, length us, event | category | flops | bytes accessed | tf_op | source)
XLA Modules:
  0.0 130.2 jit_solution(17572592214977470014)
XLA Ops:
  1.4 0.6 pad_maximum_fusion.coef_ref
  2.0 1.3 %fusion.pick_ref = bf16[24,24]{1,0:T(8,128)(2,1)} fusion(s32[24]{0:T(128)} %bitcast.1), kind=kLoop, calls=%fused_computation.1 | loop fusion | flops 1152 | bytes 1248 | tf_op jit(solution)/shard_map/convert_element_type | solution.py:266
  3.3 121.7 %clip_attention.1 = (bf16[1,192,3072]{2,1,0:T(8,128)(2,1)}, bf16[1,192,3072]{2,1,0:T(8,128)(2,1)}, bf16[1,192,3072]{2,1,0:T(8,128)(2,1)}) custom-call(s32[8]{0:T(128)} %slot_ref.1, f32[2]{0:T(128)} %pad_maximum_fusion.coef_ref, bf16[24,24]{1,0:T(8,128)(2,1)} %fusion.pick_ref, bf16[1,192,3072]{2,1,0:T(8,128)(2,1)} %q_ref.1, bf16[1,192,3072]{2,1,0:T(8,128)(2,1)} %k_ref.1, ...), custom_call_target="tpu_custom_call" | custom-call | tf_op jit(solution)/shard_map/clip_attention/pallas_call | solution.py:271
  125.0 0.0 copy-start.1
  125.0 2.5 %copy.18 = bf16[1,192,3072]{2,1,0:T(8,128)(2,1)} copy(bf16[1,192,3072]{2,1,0:T(8,128)(2,1)} %get-tuple-element.6) | data formatting | bytes 2359296
  127.5 0.0 copy-done.1
  127.5 0.0 copy-start
  127.5 1.0 copy.19
  128.5 0.7 copy-done
  129.2 1.0 copy.20
Async XLA Ops:
  125.0 2.5 %copy-start.1 = (bf16[1,192,3072]{2,1,0:T(8,128)(2,1)S(1)}, bf16[1,192,3072]{2,1,0:T(8,128)(2,1)}, u32[]{:S(2)}) copy-start(bf16[1,192,3072]{2,1,0:T(8,128)(2,1)} %get-tuple-element.7) | copy-start | bytes 3538948
  127.5 1.7 %copy-start = (bf16[1,192,3072]{2,1,0:T(8,128)(2,1)S(1)}, bf16[1,192,3072]{2,1,0:T(8,128)(2,1)}, u32[]{:S(2)}) copy-start(bf16[1,192,3072]{2,1,0:T(8,128)(2,1)} %get-tuple-element.8) | copy-start | bytes 3538948

commit v2 on v1

--- a/solution.py
+++ b/solution.py
@@ -18,11 +18,11 @@
 
 def kernel(
     nb, nc, hc, chunks,
-    slot_ref, coef_ref, pick_ref,
+    slot_ref, token_ref, time_ref,
     q_ref, k_ref, v_ref, res_ref,
     qt_ref, kt_ref, vt_ref, vel_ref,
-    out_ref, tan_ref, target_ref,
-    teach, teach_vel, send, recv, stud, dots, own_out, got_out, vel_send, vel_recv, resid, mism, goal,
+    both_ref, mism_ref, factor_ref,
+    teach, teach_vel, send, recv, stud, dots, own_out, got_out, vel_send, vel_recv, resid, mism, picks,
     part, parts,
     load_sem, send_sem, recv_sem, stud_send, stud_recv, out_send, out_recv,
     vel_ssem, vel_rsem, part_send, part_recv, write_sem,
@@ -54,7 +54,12 @@
         d = lax.rem(me + m, n)
         pl.semaphore_signal(barrier, inc=1, device_id=(d // nc, lax.rem(d, nc)), device_id_type=MESH)
 
-    pick = pick_ref[...]
+    place = lax.broadcasted_iota(jnp.int32, (1, run), 1)
+    for r in range(run):
+        picks[r:r + 1, :] = (place == token_ref[0, r]).astype(F32)
+    pick = picks[...].astype(BF16)
+    time = jnp.full((1, HEAD_DIM), time_ref[0], F32)
+    cosine, sine = jnp.cos(time), jnp.sin(time)
 
     def build(c, d):
         g, i = d // nc, lax.rem(d, nc)
@@ -91,7 +96,7 @@
     for c in range(chunks):
         @pl.loop(1, n)
         def _(m):
-            d = lax.rem(me + m, n)
+            d = lax.rem(my_b + lax.rem(m, nb), nb) * nc + lax.rem(my_c + lax.rem(m // nb * 3, nc), nc)
             build(c, d)
             pltpu.make_async_remote_copy(
                 src_ref=send.at[c, d], dst_ref=recv.at[c, me],
@@ -187,13 +192,12 @@
         waited = got_out.at[:, :, pl.ds(0, nb * cw)]
         pltpu.make_async_copy(waited, waited, out_recv.at[c]).wait()
     writes = [
-        pltpu.make_async_copy(got_out.at[0], out_ref.at[0], write_sem.at[0]),
-        pltpu.make_async_copy(got_out.at[1], tan_ref.at[0], write_sem.at[1]),
+        pltpu.make_async_copy(got_out, both_ref, write_sem.at[0]),
+        pltpu.make_async_copy(mism, mism_ref, write_sem.at[1]),
     ]
-    for write in writes:
-        write.start()
-
-    square_cos, cos_sin = coef_ref[0], coef_ref[1]
+    writes[0].start()
+
+    square_cos, cos_sin = cosine * cosine, cosine * sine
     part[...] = jnp.zeros_like(part)
 
     @pl.loop(0, width // HEAD_DIM // join)
@@ -218,18 +222,11 @@
             src_ref=part, dst_ref=parts.at[off - 1], send_sem=part_send, recv_sem=part_recv,
             device_id=(lax.rem(my_b + off, nb), my_c), device_id_type=MESH,
         ).start()
+    writes[1].start()
     pltpu.make_async_copy(parts, parts, part_recv).wait()
     whole = part[...] + jnp.sum(parts[...], axis=0)
     mean_square = jnp.sum(whole, keepdims=True) / (nb * tok * width)
-    factor = 1.0 / (jnp.sqrt(mean_square) + OFFSET)
-
-    @pl.loop(0, width // HEAD_DIM)
-    def _(h):
-        at = pl.ds(pl.multiple_of(h * HEAD_DIM, 128), HEAD_DIM)
-        goal[:, at] = (mism[:, at] * factor).astype(BF16)
-
-    last = pltpu.make_async_copy(goal, target_ref.at[0], write_sem.at[2])
-    last.start()
+    factor_ref[...] = jnp.broadcast_to(1.0 / (jnp.sqrt(mean_square) + OFFSET), factor_ref.shape)
 
     pltpu.make_async_copy(parts, parts, part_send).wait()
     sent = recv.at[:, pl.ds(0, n - 1)]
@@ -242,7 +239,12 @@
     pltpu.make_async_copy(sent, sent, vel_ssem).wait()
     for write in writes:
         write.wait()
-    last.wait()
+
+
+def finish(both_ref, mism_ref, factor_ref, out_ref, tan_ref, target_ref):
+    out_ref[0] = both_ref[0]
+    tan_ref[0] = both_ref[1]
+    target_ref[0] = (mism_ref[...] * factor_ref[0:1, 0:1]).astype(BF16)
 
 
 def local(
@@ -261,18 +263,19 @@
     slab = -(-3 * hc * run // 16) * 16
     group_width = width // nb
     heads = width // HEAD_DIM
-    cosine, sine = jnp.cos(clip_time[0]), jnp.sin(clip_time[0])
-    coef = jnp.stack([cosine * cosine, cosine * sine])
-    pick = (token_slot[0][:, None] == jnp.arange(run, dtype=jnp.int32)[None, :]).astype(BF16)
     out = jax.ShapeDtypeStruct((1, tok, width), BF16)
     anywhere = pl.BlockSpec(memory_space=pl.ANY)
     small = pl.BlockSpec(memory_space=pltpu.SMEM)
     dma = pltpu.SemaphoreType.DMA
-    return pl.pallas_call(
+    both, mism, factor = pl.pallas_call(
         functools.partial(kernel, nb, nc, hc, chunks),
-        out_shape=(out, out, out),
-        in_specs=[small, small, pl.BlockSpec(memory_space=pltpu.VMEM)] + [anywhere] * 8,
-        out_specs=(anywhere,) * 3,
+        out_shape=(
+            jax.ShapeDtypeStruct((2, tok, width), BF16),
+            jax.ShapeDtypeStruct((tok, width), F32),
+            jax.ShapeDtypeStruct((8, HEAD_DIM), F32),
+        ),
+        in_specs=[small] * 3 + [anywhere] * 8,
+        out_specs=(anywhere, anywhere, pl.BlockSpec(memory_space=pltpu.VMEM)),
         scratch_shapes=[
             pltpu.VMEM((3, clips, run, width), BF16),
             pltpu.VMEM((clips, run, width), BF16),
@@ -286,21 +289,35 @@
             pltpu.VMEM((nc, heads * run, HEAD_DIM), BF16),
             pltpu.VMEM((tok, width), BF16),
             pltpu.VMEM((tok, width), F32),
-            pltpu.VMEM((tok, width), BF16),
+            pltpu.VMEM((run, run), F32),
             pltpu.VMEM((8, HEAD_DIM), F32),
             pltpu.VMEM((nb - 1, 8, HEAD_DIM), F32),
             dma((5,)), dma, dma((chunks,)), dma, dma((chunks,)), dma, dma((chunks,)),
-            dma, dma, dma, dma, dma((3,)),
+            dma, dma, dma, dma, dma((2,)),
         ],
         compiler_params=pltpu.CompilerParams(
             collective_id=0, has_side_effects=True, vmem_limit_bytes=56 * 1024 * 1024
         ),
         name="clip_attention",
     )(
-        clip_slot, coef, pick,
+        clip_slot, token_slot, clip_time,
         query_rows, key_rows, value_rows, residual,
         query_tangent, key_tangent, value_tangent, velocity,
     )
+    step = tok // 2
+    row_block = pl.BlockSpec((1, step, width), lambda r: (0, r, 0))
+    return pl.pallas_call(
+        finish,
+        grid=(tok // step,),
+        out_shape=(out, out, out),
+        in_specs=[
+            pl.BlockSpec((2, step, width), lambda r: (0, r, 0)),
+            pl.BlockSpec((step, width), lambda r: (r, 0)),
+            pl.BlockSpec((8, HEAD_DIM), lambda r: (0, 0)),
+        ],
+        out_specs=(row_block,) * 3,
+        name="finish",
+    )(both, mism, factor)
 
 
 def solution(mesh):

time: 130 us -> 122 us (0.938)
  local copies, waits for them, and re-layouts: 5.17 us -> 0 us
  Pallas kernels: 122 us -> 120 us
  other arithmetic: 1.91 us -> 0 us
    unnamed x7 -> x0, local copies, waits for them, and re-layouts: 5.17 us -> none
    pallas_call x1, Pallas kernels: 122 us -> 117 us  [local(): pl.pallas_call(functools.partial(kernel, nb, nc, hc, chunks), out_shape=(...]
    pallas_call x0 -> x1, Pallas kernels: none -> 3.66 us  [local(): pl.pallas_call(finish, grid=(tok // step,), out_shape=(out, out, out), in...]
    convert_element_type x1 -> x0, other arithmetic: 1.32 us -> none  [local(): (token_slot[0][:, None] == jnp.arange(run, dtype=jnp.int32)[None, :]).ast...]
where the time goes in v2:
time: 122 us
  Pallas kernels  120 us (98%)
  between operations  1.29 us (1%)
    pallas_call x1, Pallas kernels, local(): pl.pallas_call(functools.partial(kernel, nb, nc, hc, chunks), out_shape=(...  117 us
    pallas_call x1, Pallas kernels, local(): pl.pallas_call(finish, grid=(tok // step,), out_shape=(out, out, out), in...  3.66 us

profile of v2, /device:TPU:0, one launch (start us, length us, event | category | flops | bytes accessed | tf_op | source)
XLA Modules:
  0.0 121.8 jit_solution(8823057781987030319)
XLA Ops:
  1.3 116.8 %clip_attention.1 = (bf16[2,192,3072]{2,1,0:T(8,128)(2,1)}, f32[192,3072]{1,0:T(8,128)}, f32[8,128]{1,0:T(8,128)}) custom-call(s32[8]{0:T(128)} %slot_ref.1, s32[1,24]{1,0:T(1,128)} %token_ref.1, f32[1]{0:T(128)S(6)} %copy.14.time_ref, bf16[1,192,3072]{2,1,0:T(8,128)(2,1)} %q_ref.1, bf16[1,192,3072]{2,1,0:T(8,128)(2,1)} %k_ref.1, ...), custom_call_target="tpu_custom_call" | custom-call | tf_op jit(solution)/shard_map/clip_attention/pallas_call | solution.py:270
  118.1 3.7 %finish.1 = (bf16[1,192,3072]{2,1,0:T(8,128)(2,1)}, bf16[1,192,3072]{2,1,0:T(8,128)(2,1)}, bf16[1,192,3072]{2,1,0:T(8,128)(2,1)}) custom-call(bf16[2,192,3072]{2,1,0:T(8,128)(2,1)} %get-tuple-element.6.both_ref, f32[192,3072]{1,0:T(8,128)} %get-tuple-element.7.mism_ref, f32[8,128]{1,0:T(8,128)} %get-tuple-element.8.factor_ref), custom_call_target="tpu_custom_call" | custom-call | tf_op jit(solution)/shard_map/finish/pallas_call | solution.py:309

commit v3 on v2

--- a/solution.py
+++ b/solution.py
@@ -89,9 +89,10 @@
                         device_id=(g, my_c), device_id_type=MESH,
                     ).start()
 
+    pl.semaphore_wait(barrier, n - 1)
+    students(0)
     for load in loads[:3]:
         load.wait()
-    pl.semaphore_wait(barrier, n - 1)
 
     for c in range(chunks):
         @pl.loop(1, n)
@@ -106,7 +107,8 @@
 
         build(c, me)
         pltpu.make_async_copy(send.at[c, me], recv.at[c, me], recv_sem.at[c]).start()
-        students(c)
+        if c > 0:
+            students(c)
 
     loads[3].wait()
 

time: 122 us -> 121 us (level)
    pallas_call x1, Pallas kernels: 117 us -> 115 us  [local(): pl.pallas_call(functools.partial(kernel, nb, nc, hc, chunks), out_shape=(...]
where the time goes in v3:
time: 121 us; the launch traced here: 120 us
  Pallas kernels  119 us (98%)
  between operations  1.29 us (1%)
    pallas_call x1, Pallas kernels, local(): pl.pallas_call(functools.partial(kernel, nb, nc, hc, chunks), out_shape=(...  115 us
    pallas_call x1, Pallas kernels, local(): pl.pallas_call(finish, grid=(tok // step,), out_shape=(out, out, out), in...  3.66 us

profile of v3, /device:TPU:0, one launch (start us, length us, event | category | flops | bytes accessed | tf_op | source)
XLA Modules:
  0.0 119.9 jit_solution(17874562327677260971)
XLA Ops:
  1.3 115.0 %clip_attention.1 = (bf16[2,192,3072]{2,1,0:T(8,128)(2,1)}, f32[192,3072]{1,0:T(8,128)}, f32[8,128]{1,0:T(8,128)}) custom-call(s32[8]{0:T(128)} %slot_ref.1, s32[1,24]{1,0:T(1,128)} %token_ref.1, f32[1]{0:T(128)S(6)} %copy.14.time_ref, bf16[1,192,3072]{2,1,0:T(8,128)(2,1)} %q_ref.1, bf16[1,192,3072]{2,1,0:T(8,128)(2,1)} %k_ref.1, ...), custom_call_target="tpu_custom_call" | custom-call | tf_op jit(solution)/shard_map/clip_attention/pallas_call | solution.py:272
  116.3 3.7 %finish.1 = (bf16[1,192,3072]{2,1,0:T(8,128)(2,1)}, bf16[1,192,3072]{2,1,0:T(8,128)(2,1)}, bf16[1,192,3072]{2,1,0:T(8,128)(2,1)}) custom-call(bf16[2,192,3072]{2,1,0:T(8,128)(2,1)} %get-tuple-element.6.both_ref, f32[192,3072]{1,0:T(8,128)} %get-tuple-element.7.mism_ref, f32[8,128]{1,0:T(8,128)} %get-tuple-element.8.factor_ref), custom_call_target="tpu_custom_call" | custom-call | tf_op jit(solution)/shard_map/finish/pallas_call | solution.py:311
